TPU v7x, 512 devices: a whole 4x4x16 slice. The times are simulated.
512 devices in a mesh: ctx: 32 (over z_lo, x), tp: 16 (over z_hi, y, core).
Axes of the slice: x: 4, y: 4, z: 16 (z_hi: 2, z_lo: 8; z = z_hi * 8 + z_lo), core: 2. Of those that a mesh axis runs over, the one named last changes fastest.
Arguments:
- query_in: bfloat16 [16384, 4096], P('ctx', 'tp'), may hold values from -6 to 6
- key_in: bfloat16 [16384, 4096], P('ctx', 'tp'), may hold values from -6 to 6
- value_in: bfloat16 [16384, 4096], P('ctx', 'tp'), may hold values from -6 to 6
- residue: float32 [4096, 16], P('tp'), may hold values from -0.125 to 0.125
- decay_rate: float32 [4096, 16], P('tp'), may hold values from 1.8310548e-05 to 0.05
- frequency: float32 [4096, 16], P('tp'), may hold values from 0 to 0.5
- skip_gain: float32 [4096], P('tp'), may hold values from -4 to 4
- out_weight: bfloat16 [4096, 4096], P('ctx', 'tp'), may hold values from -0.1875 to 0.1875
- cotangent: bfloat16 [16384, 4096], P('ctx', 'tp'), may hold values from -6 to 6
Outputs:
- layer_out: bfloat16 [16384, 4096], P('ctx', 'tp')
- grad_query: bfloat16 [16384, 4096], P('ctx', 'tp')
- grad_key: bfloat16 [16384, 4096], P('ctx', 'tp')
- grad_value: bfloat16 [16384, 4096], P('ctx', 'tp')
All inputs are finite; a program needn't handle non-finite values.
Results may differ from a plain program's by a relative error of at most 0.013.
Values may be sent and summed in bfloat16 or wider, within the bound.
A program may use at most 128 MiB of HBM per device.

v0:
```python
import math

import jax
import jax.numpy as jnp
from jax import lax
from jax.sharding import PartitionSpec as P

HIGH = lax.Precision.HIGHEST


def split_length(length):
    best = 1
    limit = math.isqrt(length)
    for candidate in range(1, limit + 1):
        if length % candidate == 0:
            best = candidate
    return best


def tables(size):
    index = jnp.arange(size, dtype=jnp.int32)
    product = index[:, None] * index[None, :] % size
    angle = product.astype(jnp.float32) * (2.0 * math.pi / size)
    return (jnp.cos(angle), jnp.sin(angle))


def twiddles(rows, cols, total):
    row_idx = jnp.arange(rows, dtype=jnp.int32)
    col_idx = jnp.arange(cols, dtype=jnp.int32)
    product = row_idx[:, None] * col_idx[None, :] % total
    angle = product.astype(jnp.float32) * (2.0 * math.pi / total)
    return (jnp.cos(angle), jnp.sin(angle))


def forward_real(signal):
    chans, length = signal.shape
    inner = split_length(length)
    outer = 2 * length // inner
    half = outer // 2
    kept = half + 1
    cos_outer, sin_outer = tables(outer)
    cos_inner, sin_inner = tables(inner)
    tw_cos, tw_sin = twiddles(kept, inner, 2 * length)
    blocks = signal.reshape(chans, half, inner)
    part_re = jnp.einsum("kn,cna->cka", cos_outer[:kept, :half], blocks, precision=HIGH)
    part_im = -jnp.einsum("kn,cna->cka", sin_outer[:kept, :half], blocks, precision=HIGH)
    turn_re = part_re * tw_cos + part_im * tw_sin
    turn_im = part_im * tw_cos - part_re * tw_sin
    spec_re = jnp.einsum("cka,am->ckm", turn_re, cos_inner, precision=HIGH) + jnp.einsum(
        "cka,am->ckm", turn_im, sin_inner, precision=HIGH
    )
    spec_im = jnp.einsum("cka,am->ckm", turn_im, cos_inner, precision=HIGH) - jnp.einsum(
        "cka,am->ckm", turn_re, sin_inner, precision=HIGH
    )
    return (spec_re, spec_im)


def inverse_real(spec_re, spec_im, length):
    chans = spec_re.shape[0]
    inner = split_length(length)
    outer = 2 * length // inner
    half = outer // 2
    kept = half + 1
    cos_outer, sin_outer = tables(outer)
    cos_inner, sin_inner = tables(inner)
    tw_cos, tw_sin = twiddles(kept, inner, 2 * length)
    row_idx = jnp.arange(kept, dtype=jnp.int32)
    weights = jnp.where((row_idx == 0) | (row_idx == half), 1.0, 2.0).astype(jnp.float32)
    part_re = jnp.einsum("ckm,ma->cka", spec_re, cos_inner, precision=HIGH) - jnp.einsum(
        "ckm,ma->cka", spec_im, sin_inner, precision=HIGH
    )
    part_im = jnp.einsum("ckm,ma->cka", spec_re, sin_inner, precision=HIGH) + jnp.einsum(
        "ckm,ma->cka", spec_im, cos_inner, precision=HIGH
    )
    turn_re = part_re * tw_cos - part_im * tw_sin
    turn_im = part_re * tw_sin + part_im * tw_cos
    cos_rows = cos_outer[:half, :kept] * weights[None, :]
    sin_rows = sin_outer[:half, :kept] * weights[None, :]
    rows = jnp.einsum("nk,cka->cna", cos_rows, turn_re, precision=HIGH) - jnp.einsum(
        "nk,cka->cna", sin_rows, turn_im, precision=HIGH
    )
    return (rows * (1.0 / (2 * length))).reshape(chans, length)


def make_filters(residue, decay_rate, frequency, length):
    positions = jnp.arange(length).astype(residue.dtype)
    summed = jnp.zeros((residue.shape[0], length), residue.dtype)
    for mode in range(residue.shape[1]):
        scaled = decay_rate[:, mode : mode + 1] * positions[None, :]
        turned = frequency[:, mode : mode + 1] * positions[None, :]
        summed = summed + residue[:, mode : mode + 1] * jnp.exp(-scaled) * jnp.cos(turned)
    return summed


def convolve(rows, kernel_re, kernel_im):
    length = rows.shape[1]
    sig_re, sig_im = forward_real(rows.astype(jnp.float32))
    prod_re = sig_re * kernel_re - sig_im * kernel_im
    prod_im = sig_re * kernel_im + sig_im * kernel_re
    return inverse_real(prod_re, prod_im, length).astype(jnp.bfloat16)


def correlate(rows, kernel_re, kernel_im):
    length = rows.shape[1]
    sig_re, sig_im = forward_real(rows.astype(jnp.float32))
    prod_re = kernel_re * sig_re + kernel_im * sig_im
    prod_im = kernel_re * sig_im - kernel_im * sig_re
    return inverse_real(prod_re, prod_im, length).astype(jnp.bfloat16)


def gating(query, key, value, grad_gated, mixed, grad_in, conv, corr, skip):
    f32 = jnp.float32
    bf16 = jnp.bfloat16
    conv, corr = lax.optimization_barrier((conv, corr))
    total = conv.astype(f32) + skip * mixed.astype(f32)
    gated = (query.astype(f32) * total).astype(bf16)
    grad_query = (grad_gated.astype(f32) * total).astype(bf16)
    grad_mixed = corr.astype(f32) + skip * grad_in.astype(f32)
    grad_key = (grad_mixed * value.astype(f32)).astype(bf16)
    grad_value = (grad_mixed * key.astype(f32)).astype(bf16)
    return (gated, grad_query, grad_key, grad_value)


def body(
    query_in, key_in, value_in, residue, decay_rate, frequency, skip_gain, out_weight, cotangent
):
    f32 = jnp.float32
    bf16 = jnp.bfloat16
    seq_rows, chans = query_in.shape
    ctx_count = lax.axis_size("ctx")
    per_dev = chans // ctx_count
    length = seq_rows * ctx_count
    first = lax.axis_index("ctx") * per_dev
    own_residue = lax.dynamic_slice_in_dim(residue, first, per_dev, 0)
    own_decay = lax.dynamic_slice_in_dim(decay_rate, first, per_dev, 0)
    own_freq = lax.dynamic_slice_in_dim(frequency, first, per_dev, 0)
    own_skip = lax.dynamic_slice_in_dim(skip_gain, first, per_dev, 0)
    kernel = make_filters(own_residue, own_decay, own_freq, length)
    kernel_re, kernel_im = forward_real(kernel)
    full_weight = lax.all_gather(out_weight, "ctx", axis=0, tiled=True)
    stacked = jnp.stack([query_in.T, key_in.T, value_in.T, cotangent.T])
    moved = lax.all_to_all(stacked, "ctx", split_axis=1, concat_axis=2, tiled=True)
    query_t, key_t, value_t, grad_t = (moved[0], moved[1], moved[2], moved[3])
    mixed_t = (key_t.astype(f32) * value_t.astype(f32)).astype(bf16)
    grad_in_t = (grad_t.astype(f32) * query_t.astype(f32)).astype(bf16)
    conv_t = convolve(mixed_t, kernel_re, kernel_im)
    corr_t = correlate(grad_in_t, kernel_re, kernel_im)
    results = gating(
        query_t, key_t, value_t, grad_t, mixed_t, grad_in_t, conv_t, corr_t, own_skip[:, None]
    )
    back = lax.all_to_all(jnp.stack(list(results)), "ctx", split_axis=2, concat_axis=1, tiled=True)
    gated = back[0].T
    grad_query = back[1].T
    grad_key = back[2].T
    grad_value = back[3].T
    projected = jnp.dot(
        lax.all_gather(gated, "tp", axis=1, tiled=True), full_weight, preferred_element_type=f32
    )
    layer_out = projected.astype(bf16)
    return (layer_out, grad_query, grad_key, grad_value)


def solution(mesh):
    return jax.shard_map(
        body,
        mesh=mesh,
        in_specs=(
            P("ctx", "tp"),
            P("ctx", "tp"),
            P("ctx", "tp"),
            P("tp", None),
            P("tp", None),
            P("tp", None),
            P("tp"),
            P("ctx", "tp"),
            P("ctx", "tp"),
        ),
        out_specs=(P("ctx", "tp"), P("ctx", "tp"), P("ctx", "tp"), P("ctx", "tp")),
        check_vma=False,
    )
```

profile of v0, /device:TPU:1, one launch (start us, length us, event | category | flops | bytes accessed | tf_op | source)
XLA Modules:
  0.0 551.3 jit_solution(12249674689194298672)
XLA Ops:
  7.2 1.1 copy.100
  8.3 1.1 copy.101
  9.4 1.1 copy.102
  10.5 1.1 copy.103
  11.8 1.8 copy.104
  13.6 15.9 %all-to-all-start = ((bf16[4,256,512]{2,0,1:T(4,128)(2,1)}), bf16[4,256,512]{2,0,1:T(4,128)(2,1)S(1)}, u32[]{:S(2)}, u32[]{:S(2)}) async-start(bf16[4,256,512]{2,0,1:T(4,128)(2,1)} %copy.104), calls=%async_computation | async-start | bytes 2097152 | tf_op jit(solution)/shard_map/all_to_all | solution.py:142
  30.2 1.0 fusion.42
  31.2 1.0 fusion.41
  32.2 30.1 %convolution_bitcast_fusion.1 = f32[8,129,128]{2,1,0:T(8,128)S(1)} fusion(f32[256,256]{0,1:T(8,128)S(1)} %fusion.42, f32[8]{0:T(128)S(1)} %get-tuple-element.97, f32[8]{0:T(128)S(1)} %get-tuple-element.102, f32[8]{0:T(128)S(1)} %get-tuple-element.65, f32[8]{0:T(128)S(1)} %get-tuple-element.83, f32[8]{0:T(128)S(1)} %get-tuple-element.116, ...), kind=kOutput, calls=%fused_computation.5 | convolution fusion | flops 215351296 | bytes 749568 | tf_op jit(solution)/shard_map/kn,cna->cka/dot_general | solution.py:45
  62.3 30.5 %fusion.1 = f32[8,129,128]{2,1,0:T(8,128)S(1)} fusion(f32[256,256]{0,1:T(8,128)S(1)} %fusion.41, f32[8]{0:T(128)S(1)} %get-tuple-element.97, f32[8]{0:T(128)S(1)} %get-tuple-element.102, f32[8]{0:T(128)S(1)} %get-tuple-element.65, f32[8]{0:T(128)S(1)} %get-tuple-element.83, f32[8]{0:T(128)S(1)} %get-tuple-element.116, f32[8]{0:T(128)S(1)} %get-tuple-element.51, ...), kind=kOutput, calls=%fused_computation.4 | convolution fusion | flops 215483392 | bytes 749568 | tf_op jit(solution)/shard_map/kn,cna->cka/dot_general | solution.py:46
  92.8 0.9 fusion.45
  93.7 1.7 fusion.46
  95.4 1.7 convolution_add_fusion.3
  98.2 0.9 convert_element_type.305
  99.0 1.5 convolution_bitcast_fusion.2
  100.5 1.4 fusion.2
  101.9 1.7 fusion.43
  103.6 1.7 fusion.44
  106.1 1.8 convert_element_type.316
  107.9 1.5 convolution_bitcast_fusion
  109.4 1.4 fusion
  110.8 0.8 fusion.48
  111.7 0.8 fusion.47
  112.6 0.9 convolution_add_fusion.4
  113.4 0.9 convolution_subtract_fusion.4
  114.3 0.9 convolution_subtract_fusion.1
  115.2 0.9 convolution_add_fusion.1
  116.1 1.5 multiply_subtract_fusion
  119.3 1.7 fusion.78
  120.9 1.7 fusion.65
  122.6 1.1 slice_convert_fusion.3
  125.4 2.8 fusion.12
  128.2 2.8 fusion.7
  131.3 1.9 convolution_subtract_fusion.2
  134.1 3.0 fusion.19
  137.1 2.8 fusion.8
  140.2 1.5 fusion.34
  142.1 15.6 %copy.116 = bf16[4,8,16384]{1,0,2:T(4,128)(2,1)} copy(bf16[4,8,16384]{2,1,0:T(8,128)(2,1)S(1)} %pad_maximum_fusion.1) | data formatting | bytes 2097152 | tf_op jit(solution)/shard_map/stack | solution.py:151
  157.7 20.6 %reshape.514 = bf16[32,2,8192]{2,1,0:T(2,128)(2,1)} reshape(bf16[16384,4,8]{2,1,0:T(4,128)(2,1)} %bitcast.257) | data formatting | bytes 2097152
  178.3 12.0 %all-to-all-start.1 = ((bf16[32,2,8192]{2,1,0:T(2,128)(2,1)}), bf16[32,2,8192]{2,1,0:T(2,128)(2,1)S(1)}, u32[]{:S(2)}, u32[]{:S(2)}) async-start(bf16[32,2,8192]{2,1,0:T(2,128)(2,1)} %reshape.514), calls=%async_computation.1 | async-start | bytes 2097152 | tf_op jit(solution)/shard_map/all_to_all | solution.py:151
  191.1 51.4 %all-to-all-done.1 = bf16[32,2,8192]{2,1,0:T(2,128)(2,1)S(1)} async-done(((bf16[32,2,8192]{2,1,0:T(2,128)(2,1)}), bf16[32,2,8192]{2,1,0:T(2,128)(2,1)S(1)}, u32[]{:S(2)}, u32[]{:S(2)}) %all-to-all-start.1) | async-done | bytes 1048608 | tf_op jit(solution)/shard_map/all_to_all | solution.py:151
  242.5 20.8 %reshape.515 = bf16[16384,4,8]{2,1,0:T(4,128)(2,1)} reshape(bf16[32,2,8192]{2,1,0:T(2,128)(2,1)S(1)} %all-to-all-done.1) | data formatting | bytes 2097152
  263.3 16.3 %copy.137 = bf16[4,8,32,512]{3,2,1,0:T(8,128)(2,1)S(1)} copy(bf16[4,8,32,512]{1,0,3,2:T(4,128)(2,1)} %bitcast.258) | data formatting | bytes 2097152 | tf_op jit(solution)/shard_map/all_to_all | solution.py:151
  279.7 0.9 copy.153
  280.8 0.8 copy.122
  283.6 113.2 %all-gather.5.cloned.1.call-done = bf16[4096,256]{1,0:T(8,128)(2,1)} async-done(((bf16[128,256]{1,0:T(8,128)(2,1)}), bf16[4096,256]{1,0:T(8,128)(2,1)}) %all-gather.5.cloned.1.call-update) | async-done | bytes 2097168 | tf_op jit(solution)/shard_map/all_gather | solution.py:140
  396.8 142.6 %all-gather.3.cloned.1.call-done = bf16[512,4096]{0,1:T(8,128)(2,1)} async-done(((bf16[512,256]{0,1:T(8,128)(2,1)}), bf16[512,4096]{0,1:T(8,128)(2,1)}) %all-gather.3.cloned.1.call-update) | async-done | bytes 4194320 | tf_op jit(solution)/shard_map/all_gather | solution.py:157
  539.4 4.9 convolution_convert_fusion
  (57 shorter events, 11.1 us)
Async XLA Ops:
  7.2 22.3 %copy-start.11 = (f32[256]{0:T(256)S(1)}, f32[256]{0:T(256)}, u32[]{:S(2)}) copy-start(f32[256]{0:T(256)} %param.15) | copy-start | bytes 3076
  7.2 22.4 %copy-start.8 = (f32[256,16]{0,1:T(8,128)S(1)}, f32[256,16]{0,1:T(8,128)}, u32[]{:S(2)}) copy-start(f32[256,16]{0,1:T(8,128)} %param.14) | copy-start | bytes 49156
  7.2 22.5 %copy-start.9 = (f32[256,16]{0,1:T(8,128)S(1)}, f32[256,16]{0,1:T(8,128)}, u32[]{:S(2)}) copy-start(f32[256,16]{0,1:T(8,128)} %param.12) | copy-start | bytes 49156
  7.2 22.5 %copy-start.10 = (f32[256,16]{0,1:T(8,128)S(1)}, f32[256,16]{0,1:T(8,128)}, u32[]{:S(2)}) copy-start(f32[256,16]{0,1:T(8,128)} %param.13) | copy-start | bytes 49156
  13.6 83.5 %all-to-all-start = ((bf16[4,256,512]{2,0,1:T(4,128)(2,1)}), bf16[4,256,512]{2,0,1:T(4,128)(2,1)S(1)}, u32[]{:S(2)}, u32[]{:S(2)}) async-start(bf16[4,256,512]{2,0,1:T(4,128)(2,1)} %copy.104), calls=%async_computation | async-start | bytes 2097152 | tf_op jit(solution)/shard_map/all_to_all | solution.py:142
  31.2 31.1 %copy-start.5 = (f32[256,256]{0,1:T(8,128)}, f32[256,256]{0,1:T(8,128)S(1)}, u32[]{:S(2)}) copy-start(f32[256,256]{0,1:T(8,128)S(1)} %fusion.42) | copy-start | bytes 786436
  32.2 30.1 %copy-start.6 = (f32[256,256]{0,1:T(8,128)}, f32[256,256]{0,1:T(8,128)S(1)}, u32[]{:S(2)}) copy-start(f32[256,256]{0,1:T(8,128)S(1)} %fusion.41) | copy-start | bytes 786436
  99.0 6.3 %copy-start.7 = (bf16[1,8,32,512]{3,1,2,0:T(8,128)(2,1)S(1)}, bf16[1,8,32,512]{3,1,2,0:T(8,128)(2,1)}, u32[]{:S(2)}) copy-start(bf16[1,8,32,512]{3,1,2,0:T(8,128)(2,1)} %get-tuple-element.48) | copy-start | bytes 786436
  107.9 4.7 copy-start.2
  107.9 5.5 %copy-start.1 = (f32[8,129,128]{2,1,0:T(8,128)S(1)}, f32[8,129,128]{2,1,0:T(8,128)}, u32[]{:S(2)}) copy-start(f32[8,129,128]{2,1,0:T(8,128)} %fusion.44) | copy-start | bytes 1585156
  112.5 3.5 copy-start.3
  112.6 3.5 copy-start.4
  124.6 8.7 %copy-start = (f32[8,129,128]{2,1,0:T(8,128)S(1)}, f32[8,129,128]{2,1,0:T(8,128)}, u32[]{:S(2)}) copy-start(f32[8,129,128]{2,1,0:T(8,128)} %fusion.65) | copy-start | bytes 1585156
  178.3 64.2 %all-to-all-start.1 = ((bf16[32,2,8192]{2,1,0:T(2,128)(2,1)}), bf16[32,2,8192]{2,1,0:T(2,128)(2,1)S(1)}, u32[]{:S(2)}, u32[]{:S(2)}) async-start(bf16[32,2,8192]{2,1,0:T(2,128)(2,1)} %reshape.514), calls=%async_computation.1 | async-start | bytes 2097152 | tf_op jit(solution)/shard_map/all_to_all | solution.py:151
  190.3 206.5 %all-gather.5.cloned.1.call-start = ((), (), s32[]{:S(2)}) async-start(), calls=%async_computation.3 | async-start | bytes 2162688 | tf_op jit(solution)/shard_map/all_gather | solution.py:140
  191.1 348.3 %all-gather.3.cloned.1.call-start = ((), (), s32[]{:S(2)}) async-start(), calls=%async_computation.2 | async-start | bytes 4456448 | tf_op jit(solution)/shard_map/all_gather | solution.py:157
Sparse Core Ops, SparseCore 0:
  193.2 203.5 all-gather.4
  400.7 138.6 all-gather.2
where the time goes:
time: 562 us; the launch traced here: 551 us
  waiting for transfers between devices  308 us (55%)
  matrix products  106 us (19%)
  local copies, waits for them, and re-layouts  88.3 us (16%)
  starting transfers between devices  28 us (5%)
  between operations  14.7 us (3%)
  other arithmetic  6.22 us (1%)
    all_gather x1, waiting for transfers between devices, body(): lax.all_gather(gated, 'tp', axis=1, tiled=True)  143 us
    all_gather x1, waiting for transfers between devices, body(): full_weight = lax.all_gather(out_weight, 'ctx', axis=0, tiled=True)  113 us
    all_to_all x1, waiting for transfers between devices, body(): lax.all_to_all(jnp.stack(list(results)), 'ctx', split_axis=2, concat_axis...  51.4 us
    unnamed x35, local copies, waits for them, and re-layouts  48.7 us
    dot_general x3, matrix products, forward_real(): jnp.einsum('kn,cna->cka', sin_outer[:kept, :half], blocks, precision=HIGH)  33.3 us
    dot_general x3, matrix products, forward_real(): jnp.einsum('kn,cna->cka', cos_outer[:kept, :half], blocks, precision=HIGH)  33.1 us
    all_to_all x1, local copies, waits for them, and re-layouts, body(): lax.all_to_all(jnp.stack(list(results)), 'ctx', split_axis=2, concat_axis...  16.3 us
    all_to_all x1, starting transfers between devices, body(): lax.all_to_all(stacked, 'ctx', split_axis=1, concat_axis=2, tiled=True)  15.9 us
  transfers between devices with their start and end apart: 4, of which 3 were waited for; matrix products, arithmetic and copies ran while one was open for 20% of the time, Pallas kernels for 0%

commit v1 on v0

v1 whole, which is shorter than its diff:
```python
import jax
import jax.numpy as jnp
from jax import lax
from jax.experimental import pallas as pl
from jax.experimental.pallas import tpu as pltpu
from jax.sharding import PartitionSpec as P

F32 = jnp.float32
BF16 = jnp.bfloat16
MESH = pl.DeviceIdType.MESH

NZ, NX, NY = 8, 4, 4
ROWS, LANES, HALVES = 512, 128, 2
STEP, LOS, SUBS = 16, 4, 8
STRETCH = STEP * LOS
GROUPS, PER = 4, 4
PIECES = 4
PIECE = ROWS // PIECES
FIRST, CHUNK, WIDE, DEVICE, COLUMN, GAIN = range(6)


def cmul(ar, ai, br, bi):
    return ar * br - ai * bi, ar * bi + ai * br


def shifted(value, amount, back):
    row = lax.broadcasted_iota(jnp.int32, (SUBS, LANES), 0)
    if back:
        return jnp.where(row < SUBS - amount, pltpu.roll(value, SUBS - amount, 0), 0.0)
    return jnp.where(row >= amount, pltpu.roll(value, amount, 0), 0.0)


def kernel(
    q_ref,
    k_ref,
    v_ref,
    g_ref,
    w_ref,
    par_ref,
    skip_ref,
    out_ref,
    gq_ref,
    gk_ref,
    gv_ref,
    mixed,
    grad_in,
    conv,
    partial,
    chunk_state,
    entry,
    zstate,
    powers,
    taps,
    wide_pow,
    own_state,
    recv_x,
    column,
    recv_z,
    prefix,
    entry_in,
    weights,
    gated,
    total,
    w_send_z,
    w_send_x,
    w_recv,
    s_send,
    x_recv,
    z_recv,
    p_recv,
    g_send,
    f_send,
    g_recv,
):
    ctx = lax.axis_index("ctx")
    tp = lax.axis_index("tp")
    zlo, x = lax.div(ctx, NX), lax.rem(ctx, NX)
    zhi, y, core = lax.div(tp, 2 * NY), lax.rem(lax.div(tp, 2), NY), lax.rem(tp, 2)

    def at_x(step):
        return (zlo * NX + lax.rem(x + step, NX), tp)

    def at_z(step):
        return (lax.rem(zlo + step, NZ) * NX + x, tp)

    def tp_of(h, yy, c):
        return (h * NY + yy) * 2 + c

    def at_y(step):
        return (ctx, tp_of(zhi, lax.rem(y + step, NY), core))

    far = (ctx, tp_of(1 - zhi, y, core))
    sibling = (ctx, tp_of(zhi, y, 1 - core))

    barrier = pltpu.get_barrier_semaphore()
    partners = [at_x(i) for i in range(1, NX)] + [at_z(i) for i in range(1, NZ)]
    partners += [at_y(i) for i in range(1, NY)] + [far, sibling]
    for partner in partners:
        pl.semaphore_signal(barrier, inc=1, device_id=partner, device_id_type=MESH)
    pl.semaphore_wait(barrier, len(partners))

    def copy(src, dst, send, recv, device):
        return pltpu.make_async_remote_copy(
            src_ref=src, dst_ref=dst, send_sem=send, recv_sem=recv,
            device_id=device, device_id_type=MESH,
        )

    def w_copy_z(step, right):
        block = (zlo - step if right else zlo + step) * NX + x
        slot = weights.at[block]
        to = (ctx + NX, tp) if right else (ctx - NX, tp)
        return copy(slot, slot, w_send_z.at[0 if right else 1, step], w_recv.at[block], to)

    def w_copy_x(z, step):
        block = z * NX + x
        slot = weights.at[block]
        return copy(slot, slot, w_send_x.at[z, step], w_recv.at[block], at_x(step))

    def w_wait_recv(block):
        slot = weights.at[block]
        copy(slot, slot, w_send_x.at[0, 0], w_recv.at[block], at_x(1)).wait_recv()

    def w_right(step):
        return jnp.logical_and(zlo - step >= 0, zlo < NZ - 1)

    def w_left(step):
        return jnp.logical_and(zlo + step < NZ, zlo > 0)

    def w_step(step):
        if step:
            @pl.when(zlo - step >= 0)
            def _():
                w_wait_recv((zlo - step) * NX + x)

            @pl.when(zlo + step < NZ)
            def _():
                w_wait_recv((zlo + step) * NX + x)

        @pl.when(w_right(step))
        def _():
            w_copy_z(step, True).start()

        @pl.when(w_left(step))
        def _():
            w_copy_z(step, False).start()

        @pl.when(zlo - step >= 0)
        def _():
            for i in range(1, NX):
                w_copy_x(zlo - step, i).start()

        if step:
            @pl.when(zlo + step < NZ)
            def _():
                for i in range(1, NX):
                    w_copy_x(zlo + step, i).start()

    weights[ctx] = w_ref[...]
    w_step(0)

    def make_tables(h):
        def group(mg, acc):
            one = par_ref[h, mg, FIRST]
            ar, ai = one[:PER], one[PER:]
            gain = par_ref[h, mg, GAIN][:PER]
            pr, pi = jnp.ones_like(ar), jnp.zeros_like(ai)
            acc = list(acc)
            for p in range(STEP + 1):
                powers[h, mg, p] = jnp.concatenate([pr, pi], axis=0)
                if p < STEP:
                    acc[p] = acc[p] + gain * pr
                    pr, pi = cmul(pr, pi, ar, ai)
            return tuple(acc)

        acc = lax.fori_loop(0, GROUPS, group, (jnp.zeros((PER, LANES), F32),) * STEP)
        for p in range(STEP):
            taps[h, pl.ds(p, 1)] = jnp.sum(acc[p], axis=0, keepdims=True)

    def make_wide(index, carry):
        h, mg = lax.div(index, GROUPS), lax.rem(index, GROUPS)
        row = lax.broadcasted_iota(jnp.int32, (SUBS, LANES), 0)
        for back in (False, True):
            for i in range(PER):
                start = jnp.where(row == (SUBS - 1 if back else 0), 1.0, 0.0).astype(F32)
                re, im = scan_wide(h, mg, i, start, jnp.zeros_like(start), back)
                wide_pow[int(back), h, mg, i] = re
                wide_pow[int(back), h, mg, PER + i] = im
        return carry

    def scan_wide(h, mg, i, re, im, back):
        br = par_ref[h, mg, WIDE, pl.ds(i, 1)]
        bi = par_ref[h, mg, WIDE, pl.ds(PER + i, 1)]
        for amount in (1, 2, 4):
            sr, si = cmul(br, bi, shifted(re, amount, back), shifted(im, amount, back))
            re, im = re + sr, im + si
            if amount < 4:
                br, bi = cmul(br, bi, br, bi)
        return re, im

    def rows_at(lo, b):
        return pl.ds(lo * STEP + b, SUBS, stride=STRETCH)

    def state_in(back, signal, index):
        h, mg = lax.div(index, GROUPS), lax.rem(index, GROUPS)
        way = int(back)
        acc = [[None] * LOS for _ in range(2 * PER)]
        for p in range(STEP):
            b = p if back else STEP - 1 - p
            values = [signal[h, rows_at(lo, b)] for lo in range(LOS)]
            for r in range(2 * PER):
                if p == 0:
                    for lo in range(LOS):
                        acc[r][lo] = values[lo] if r < PER else jnp.zeros_like(values[lo])
                    continue
                coef = powers[h, mg, p, pl.ds(r, 1)]
                for lo in range(LOS):
                    acc[r][lo] = acc[r][lo] + coef * values[lo]
        for i in range(PER):
            cr = par_ref[h, mg, CHUNK, pl.ds(i, 1)]
            ci = par_ref[h, mg, CHUNK, pl.ds(PER + i, 1)]
            order = list(range(LOS))[::-1] if back else list(range(LOS))
            ur, ui = acc[i][order[0]], acc[PER + i][order[0]]
            for lo in order[1:]:
                ur, ui = cmul(cr, ci, ur, ui)
                ur, ui = ur + acc[i][lo], ui + acc[PER + i][lo]
            for lo in range(LOS):
                chunk_state[way, h, mg, i, lo] = acc[i][lo]
                chunk_state[way, h, mg, PER + i, lo] = acc[PER + i][lo]
            er, ei = scan_wide(h, mg, i, shifted(ur, 1, back), shifted(ui, 1, back), back)
            entry[way, h, mg, i] = er
            entry[way, h, mg, PER + i] = ei
            br = par_ref[h, mg, WIDE, pl.ds(i, 1)]
            bi = par_ref[h, mg, WIDE, pl.ds(PER + i, 1)]
            dr, di = cmul(br, bi, er, ei)
            last = 0 if back else SUBS - 1
            own_state[mg, h, pl.ds(way * 8 + i, 1)] = (dr + ur)[last : last + 1]
            own_state[mg, h, pl.ds(way * 8 + PER + i, 1)] = (di + ui)[last : last + 1]

    def inside(back, signal, h):
        coef = [taps[h, pl.ds(p, 1)] for p in range(STEP)]
        for lo in range(LOS):
            values = [signal[h, rows_at(lo, b)] for b in range(STEP)]
            for b in range(STEP):
                js = range(b, STEP) if back else range(b + 1)
                acc = None
                for j in js:
                    term = coef[abs(b - j)] * values[j]
                    acc = term if acc is None else acc + term
                partial[int(back), h, b, lo] = acc

    def inject(back, h):
        way = int(back)

        def prepare(mg, carry):
            for i in range(PER):
                pr = entry_in[mg, h, pl.ds(way * 8 + i, 1)]
                pi = entry_in[mg, h, pl.ds(way * 8 + PER + i, 1)]
                er, ei = cmul(wide_pow[way, h, mg, i], wide_pow[way, h, mg, PER + i], pr, pi)
                zr, zi = er + entry[way, h, mg, i], ei + entry[way, h, mg, PER + i]
                cr = par_ref[h, mg, CHUNK, pl.ds(i, 1)]
                ci = par_ref[h, mg, CHUNK, pl.ds(PER + i, 1)]
                gain = par_ref[h, mg, GAIN, pl.ds(i, 1)]
                order = list(range(LOS))[::-1] if back else list(range(LOS))
                for n, lo in enumerate(order):
                    zstate[mg, i, lo] = gain * zr
                    zstate[mg, PER + i, lo] = -(gain * zi)
                    if n < LOS - 1:
                        zr, zi = cmul(cr, ci, zr, zi)
                        zr = zr + chunk_state[way, h, mg, i, lo]
                        zi = zi + chunk_state[way, h, mg, PER + i, lo]
            return carry

        lax.fori_loop(0, GROUPS, prepare, 0)
        for b0 in range(0, STEP, 4):

            def group(mg, acc):
                acc = list(acc)
                for r in range(2 * PER):
                    states = [zstate[mg, r, lo] for lo in range(LOS)]
                    for n in range(4):
                        b = b0 + n
                        coef = powers[h, mg, STEP - b if back else b + 1, pl.ds(r, 1)]
                        for lo in range(LOS):
                            acc[n * LOS + lo] = acc[n * LOS + lo] + coef * states[lo]
                return tuple(acc)

            start = tuple(partial[way, h, b0 + n, lo] for n in range(4) for lo in range(LOS))
            acc = lax.fori_loop(0, GROUPS, group, start)
            for n in range(4):
                for lo in range(LOS):
                    conv[h, rows_at(lo, b0 + n)] = acc[n * LOS + lo]

    def lanes(h):
        return pl.ds(h * LANES, LANES)

    def prepare_rows(h):
        for r0 in range(0, ROWS, 128):
            rows = pl.ds(r0, 128)
            prod = k_ref[rows, lanes(h)].astype(F32) * v_ref[rows, lanes(h)].astype(F32)
            mixed[h, rows] = prod.astype(BF16).astype(F32)
            prod = g_ref[rows, lanes(h)].astype(F32) * q_ref[rows, lanes(h)].astype(F32)
            grad_in[h, rows] = prod.astype(BF16).astype(F32)

    def gate_forward(h):
        skip = skip_ref[:, lanes(h)]
        for r0 in range(0, ROWS, 128):
            rows = pl.ds(r0, 128)
            summed = conv[h, rows].astype(BF16).astype(F32) + skip * mixed[h, rows]
            gated[tp, h, rows] = (q_ref[rows, lanes(h)].astype(F32) * summed).astype(BF16)
            gq_ref[rows, lanes(h)] = (g_ref[rows, lanes(h)].astype(F32) * summed).astype(BF16)

    def gate_backward(h):
        skip = skip_ref[:, lanes(h)]
        for r0 in range(0, ROWS, 128):
            rows = pl.ds(r0, 128)
            summed = conv[h, rows].astype(BF16).astype(F32) + skip * grad_in[h, rows]
            gk_ref[rows, lanes(h)] = (summed * v_ref[rows, lanes(h)].astype(F32)).astype(BF16)
            gv_ref[rows, lanes(h)] = (summed * k_ref[rows, lanes(h)].astype(F32)).astype(BF16)

    for h in range(HALVES):
        make_tables(h)
        prepare_rows(h)

    def forward_states(index, carry):
        state_in(False, mixed, index)
        return carry

    def backward_states(index, carry):
        state_in(True, grad_in, index)
        return carry

    lax.fori_loop(0, HALVES * GROUPS, forward_states, 0)
    lax.fori_loop(0, HALVES * GROUPS, backward_states, 0)
    lax.fori_loop(0, HALVES * GROUPS, make_wide, 0)

    round_x = [
        copy(own_state.at[lax.rem(x + i, NX)], recv_x.at[x], s_send.at[0, i], x_recv.at[x], at_x(i))
        for i in range(1, NX)
    ]
    for c in round_x:
        c.start()
    recv_x[x] = own_state[x]
    w_step(1)
    inside(False, mixed, 0)
    for i in range(1, NX):
        src = lax.rem(x + NX - i, NX)
        copy(own_state.at[0], recv_x.at[src], s_send.at[0, i], x_recv.at[src], at_x(i)).wait_recv()

    def cpack(value):
        return value[:PER], value[PER:]

    def step_on(power, h, state, added):
        re, im = cmul(*cpack(par_ref[h, x, power]), *cpack(state))
        return jnp.concatenate([re, im], axis=0) + added

    for h in range(HALVES):
        state = recv_x[0, h, pl.ds(0, 8)]
        for i in range(1, NX):
            state = step_on(DEVICE, h, state, recv_x[i, h, pl.ds(0, 8)])
        column[0, h] = state
        state = recv_x[NX - 1, h, pl.ds(8, 8)]
        for i in range(NX - 2, -1, -1):
            state = step_on(DEVICE, h, state, recv_x[i, h, pl.ds(8, 8)])
        column[1, h] = state

    round_z = []
    for i in range(1, NZ):
        way = jnp.where(zlo + i < NZ, 0, 1)
        round_z.append(
            copy(column.at[way], recv_z.at[zlo], s_send.at[1, i], z_recv.at[zlo], at_z(i))
        )
    for c in round_z:
        c.start()
    recv_z[zlo] = jnp.zeros_like(recv_z[zlo])
    inside(False, mixed, 1)
    w_step(2)
    inside(True, grad_in, 0)
    inside(True, grad_in, 1)
    for i in range(1, NZ):
        src = lax.rem(zlo + NZ - i, NZ)
        copy(column.at[0], recv_z.at[src], s_send.at[1, i], z_recv.at[src], at_z(i)).wait_recv()

    for h in range(HALVES):
        state = jnp.zeros((2 * PER, LANES), F32)
        for z in range(NZ):
            state = jnp.where(z < zlo, step_on(COLUMN, h, state, recv_z[z, h]), state)
        for i in range(NX):
            prefix[i, h, pl.ds(0, 8)] = state
            if i < NX - 1:
                state = step_on(DEVICE, h, state, recv_x[i, h, pl.ds(0, 8)])
        state = jnp.zeros((2 * PER, LANES), F32)
        for z in range(NZ - 1, -1, -1):
            state = jnp.where(z > zlo, step_on(COLUMN, h, state, recv_z[z, h]), state)
        for i in range(NX - 1, -1, -1):
            prefix[i, h, pl.ds(8, 8)] = state
            if i > 0:
                state = step_on(DEVICE, h, state, recv_x[i, h, pl.ds(8, 8)])

    round_p = [
        copy(prefix.at[lax.rem(x + i, NX)], entry_in.at[x], s_send.at[2, i], p_recv.at[x], at_x(i))
        for i in range(1, NX)
    ]
    for c in round_p:
        c.start()
    entry_in[x] = prefix[x]
    w_step(3)
    for i in range(1, NX):
        src = lax.rem(x + NX - i, NX)
        copy(prefix.at[0], entry_in.at[src], s_send.at[2, i], p_recv.at[src], at_x(i)).wait_recv()

    def piece(block, h, n):
        return gated.at[block, h, pl.ds(n * PIECE, PIECE)]

    def half(block, h):
        return gated.at[block, h]

    sends = []

    def send(src, sem, recv, to):
        c = copy(src, src, sem, recv, to)
        c.start()
        sends.append(c)

    for h in range(HALVES):
        inject(False, h)
        gate_forward(h)
        for n in range(PIECES):
            send(piece(tp, h, n), g_send.at[h, n], g_recv.at[tp, h, n], far)
        for i in range(1, NY):
            send(half(tp, h), g_send.at[h, PIECES + i - 1], g_recv.at[tp, h, 0], at_y(i))
        send(half(tp, h), g_send.at[h, PIECES + 3], g_recv.at[tp, h, 0], sibling)
        w_step(4 + h)

    for h in range(HALVES):
        inject(True, h)
        gate_backward(h)
        if h == 0:
            w_step(6)
    w_step(7)

    far_tp = far[1]

    def wait_half(block, h):
        copy(half(block, h), half(block, h), g_send.at[0, 0], g_recv.at[block, h, 0], far).wait_recv()

    def wait_piece(block, h, n):
        part = piece(block, h, n)
        copy(part, part, g_send.at[0, 0], g_recv.at[block, h, n], far).wait_recv()

    for h in range(HALVES):
        for i in range(1, NY):
            block = tp_of(zhi, lax.rem(y + NY - i, NY), core)
            wait_half(block, h)
            send(half(block, h), f_send.at[0, h, i], g_recv.at[block, h, 0], sibling)

    def pass_on(h, n):
        wait_piece(far_tp, h, n)
        for i in range(1, NY):
            to = at_y(i)
            send(piece(far_tp, h, n), f_send.at[1 + n, h, i], g_recv.at[far_tp, h, n], to)
        send(piece(far_tp, h, n), f_send.at[1 + n, h, 0], g_recv.at[far_tp, h, n], sibling)

    def pass_core(h, n):
        for i in range(1, NY):
            block = tp_of(1 - zhi, lax.rem(y + NY - i, NY), core)
            wait_piece(block, h, n)
            send(
                piece(block, h, n), f_send.at[1 + PIECES + n, h, i], g_recv.at[block, h, n], sibling
            )

    def near_product():
        for h in range(HALVES):
            for i in range(NY):
                wait_half(tp_of(zhi, i, 1 - core), h)

        for z in range(NZ):
            for i in range(1, NX):
                w_wait_recv(z * NX + lax.rem(x + i, NX))

        def rows_of(n, carry):
            rows = pl.ds(pl.multiple_of(n * PIECE, PIECE), PIECE)
            left = jnp.concatenate(
                [gated[zhi * 8 + j, h, rows] for j in range(8) for h in range(HALVES)], axis=1
            )
            right = jnp.concatenate([weights[zhi * 16 + j] for j in range(16)], axis=0)
            total[rows] = jnp.dot(left, right, preferred_element_type=F32)
            return carry

        lax.fori_loop(0, PIECES, rows_of, 0)

    def far_product(h, n):
        for i in range(NY):
            wait_piece(tp_of(1 - zhi, i, 1 - core), h, n)
        first = (1 - zhi) * 8
        rows = pl.ds(n * PIECE, PIECE)
        left = jnp.concatenate([gated[first + j, h, rows] for j in range(8)], axis=1)
        right = jnp.concatenate([weights[2 * (first + j) + h] for j in range(8)], axis=0)
        summed = total[rows] + jnp.dot(left, right, preferred_element_type=F32)
        if h == HALVES - 1:
            out_ref[rows] = summed.astype(BF16)
        else:
            total[rows] = summed

    order = [(h, n) for h in range(HALVES) for n in range(PIECES)]
    near_at = 5
    for s in range(len(order) + 2):
        if s < len(order):
            pass_on(*order[s])
        if s == near_at:
            near_product()
            for t in range(s - 1):
                far_product(*order[t])
        if 1 <= s <= len(order):
            pass_core(*order[s - 1])
        if s > near_at:
            far_product(*order[s - 2])

    for c in sends + round_x + round_z + round_p:
        c.wait_send()
    for step in range(NZ):
        @pl.when(w_right(step))
        def _():
            w_copy_z(step, True).wait_send()

        @pl.when(w_left(step))
        def _():
            w_copy_z(step, False).wait_send()

    for z in range(NZ):
        for i in range(1, NX):
            w_copy_x(z, i).wait_send()


def body(
    query_in, key_in, value_in, residue, decay_rate, frequency, skip_gain, out_weight, cotangent
):
    def arranged(array):
        return array.reshape(HALVES, LANES, GROUPS, PER).transpose(0, 2, 3, 1)

    decay, freq = arranged(decay_rate), arranged(frequency)
    count = jnp.array([1.0, STEP, STRETCH, ROWS, ROWS * NX], F32).reshape(5, 1, 1)
    size = jnp.exp(-(decay[:, :, None] * count))
    angle = freq[:, :, None] * count
    table = jnp.concatenate([size * jnp.cos(angle), size * jnp.sin(angle)], axis=3)
    gain = jnp.concatenate([arranged(residue)] * 2, axis=2)[:, :, None]
    params = jnp.concatenate([table, gain], axis=2)

    vmem = pl.BlockSpec(memory_space=pltpu.VMEM)
    stream = jax.ShapeDtypeStruct((ROWS, HALVES * LANES), BF16)
    blocks = lax.axis_size("tp")
    sem = pltpu.SemaphoreType.DMA
    tile = (SUBS, LANES)
    return pl.pallas_call(
        kernel,
        out_shape=(stream,) * 4,
        in_specs=[vmem] * 7,
        out_specs=(vmem,) * 4,
        scratch_shapes=[
            pltpu.VMEM((HALVES, ROWS, LANES), F32),
            pltpu.VMEM((HALVES, ROWS, LANES), F32),
            pltpu.VMEM((HALVES, ROWS, LANES), F32),
            pltpu.VMEM((2, HALVES, STEP, LOS) + tile, F32),
            pltpu.VMEM((2, HALVES, GROUPS, 2 * PER, LOS) + tile, F32),
            pltpu.VMEM((2, HALVES, GROUPS, 2 * PER) + tile, F32),
            pltpu.VMEM((GROUPS, 2 * PER, LOS) + tile, F32),
            pltpu.VMEM((HALVES, GROUPS, STEP + 1, 2 * PER, LANES), F32),
            pltpu.VMEM((HALVES, STEP, LANES), F32),
            pltpu.VMEM((2, HALVES, GROUPS, 2 * PER) + tile, F32),
            pltpu.VMEM((GROUPS, HALVES, 4 * PER, LANES), F32),
            pltpu.VMEM((NX, HALVES, 4 * PER, LANES), F32),
            pltpu.VMEM((2, HALVES, 2 * PER, LANES), F32),
            pltpu.VMEM((NZ, HALVES, 2 * PER, LANES), F32),
            pltpu.VMEM((NX, HALVES, 4 * PER, LANES), F32),
            pltpu.VMEM((GROUPS, HALVES, 4 * PER, LANES), F32),
            pltpu.VMEM((NZ * NX, 128, HALVES * LANES), BF16),
            pltpu.VMEM((blocks, HALVES, ROWS, LANES), BF16),
            pltpu.VMEM((ROWS, HALVES * LANES), F32),
            sem((2, NZ)),
            sem((NZ, NX)),
            sem((NZ * NX,)),
            sem((3, NZ)),
            sem((NX,)),
            sem((NZ,)),
            sem((NX,)),
            sem((HALVES, PIECES + 4)),
            sem((1 + 2 * PIECES, HALVES, 4)),
            sem((blocks, HALVES, PIECES)),
        ],
        compiler_params=pltpu.CompilerParams(
            collective_id=0, has_side_effects=True, vmem_limit_bytes=48 * 1024 * 1024
        ),
    )(query_in, key_in, value_in, cotangent, out_weight, params, skip_gain.reshape(1, -1))


def solution(mesh):
    return jax.shard_map(
        body,
        mesh=mesh,
        in_specs=(
            P("ctx", "tp"),
            P("ctx", "tp"),
            P("ctx", "tp"),
            P("tp", None),
            P("tp", None),
            P("tp", None),
            P("tp"),
            P("ctx", "tp"),
            P("ctx", "tp"),
        ),
        out_specs=(P("ctx", "tp"), P("ctx", "tp"), P("ctx", "tp"), P("ctx", "tp")),
        check_vma=False,
    )
```

time: 562 us -> 100 us (0.18); the launches traced: 551 us -> 99.7 us
  waiting for transfers between devices: 308 us -> 0 us
  matrix products: 106 us -> 0 us
  Pallas kernels: 0 us -> 92.1 us
  local copies, waits for them, and re-layouts: 88.3 us -> 6.1 us
  starting transfers between devices: 28 us -> 0 us
  between operations: 14.7 us -> 0.77 us
    all_gather x2 -> x0, waiting for transfers between devices: 256 us -> none  [the longest x1 143 us: body(): lax.all_gather(gated, 'tp', axis=1, tiled=True)]
    dot_general x31 -> x0, matrix products: 106 us -> none  [the longest x3 33.3 us: forward_real(): jnp.einsum('kn,cna->cka', sin_outer[:kept, :half], blocks, precision=HIGH)]
    pallas_call x0 -> x1, Pallas kernels: none -> 92.1 us  [body(): pl.pallas_call(kernel, out_shape=(stream,) * 4, in_specs=[vmem] * 7, out_...]
    all_to_all x2 -> x0, waiting for transfers between devices: 51.4 us -> none  [the longest x1 51.4 us: body(): lax.all_to_all(jnp.stack(list(results)), 'ctx', split_axis=2, concat_axis...]
    unnamed x35 -> x22, local copies, waits for them, and re-layouts: 48.7 us -> 5.31 us
    all_to_all x2 -> x0, starting transfers between devices: 27.9 us -> none  [the longest x1 15.9 us: body(): lax.all_to_all(stacked, 'ctx', split_axis=1, concat_axis=2, tiled=True)]
    another operation x2 -> x0, local copies, waits for them, and re-layouts: 17.4 us -> none  [the longest x1 15.6 us: body(): jnp.stack(list(results))]
    all_to_all x2 -> x0, local copies, waits for them, and re-layouts: 16.5 us -> none  [the longest x1 16.3 us: body(): lax.all_to_all(jnp.stack(list(results)), 'ctx', split_axis=2, concat_axis...]
  transfers between devices with their start and end apart: 4 -> 0, of which waited for: 3 -> 0; matrix products, arithmetic and copies ran while one was open for 20% -> 0% of each run, Pallas kernels for 0% -> 0%
where the time goes in v1:
time: 100 us; the launch traced here: 99.7 us
  Pallas kernels  92.1 us (92%)
  local copies, waits for them, and re-layouts  6.1 us (6%)
    pallas_call x1, Pallas kernels, body(): pl.pallas_call(kernel, out_shape=(stream,) * 4, in_specs=[vmem] * 7, out_...  92.1 us
    unnamed x22, local copies, waits for them, and re-layouts  5.31 us

profile of v1, /device:TPU:1, one launch (start us, length us, event | category | flops | bytes accessed | tf_op | source)
XLA Modules:
  0.0 99.7 jit_solution(15006923560803662563)
XLA Ops:
  0.6 0.0 copy-start.6
  0.6 0.0 copy-start.7
  0.7 0.0 copy-start.8
  0.7 0.7 reshape.25
  1.4 0.0 copy-start.2
  1.5 0.0 copy-done.6
  1.5 0.0 copy-done.7
  1.5 0.0 copy-done.8
  1.5 0.0 copy-start
  1.6 0.0 copy-start.1
  1.6 0.7 fusion
  2.2 0.0 copy-start.5
  2.3 0.1 copy-done.2
  2.4 0.1 copy-done
  2.5 0.1 copy-done.1
  2.6 0.4 copy-done.5
  3.0 0.0 copy-start.3
  3.0 0.9 copy-done.3
  3.9 0.0 copy-start.4
  3.9 0.8 copy-done.4
  4.8 92.1 %shard_map.129 = (bf16[512,256]{1,0:T(8,128)(2,1)S(1)}, bf16[512,256]{1,0:T(8,128)(2,1)S(1)}, bf16[512,256]{1,0:T(8,128)(2,1)S(1)}, bf16[512,256]{1,0:T(8,128)(2,1)S(1)}) custom-call(bf16[512,256]{1,0:T(8,128)(2,1)S(1)} %copy-done, bf16[512,256]{1,0:T(8,128)(2,1)S(1)} %copy-done.1, bf16[512,256]{1,0:T(8,128)(2,1)S(1)} %copy-done.2, ...), custom_call_target="tpu_custom_call" | custom-call | tf_op jit(solution)/shard_map/pallas_call | solution.py:553
  96.9 0.7 copy.27
  97.6 0.7 copy.28
  98.3 0.7 copy.29
  99.0 0.7 copy.30
  (6 shorter events, 0.1 us)
Async XLA Ops:
  0.6 0.8 copy-start.6
  0.6 0.8 copy-start.7
  0.7 0.9 copy-start.8
  1.4 1.0 copy-start.2
  1.5 1.0 copy-start
  1.6 1.0 %copy-start.1 = (bf16[512,256]{1,0:T(8,128)(2,1)S(1)}, bf16[512,256]{1,0:T(8,128)(2,1)}, u32[]{:S(2)}) copy-start(bf16[512,256]{1,0:T(8,128)(2,1)} %k_ref.1) | copy-start | bytes 786436
  2.2 0.7 copy-start.5
  3.0 0.9 copy-start.3
  3.9 0.8 copy-start.4

commit v2 on v1

--- a/solution.py
+++ b/solution.py
@@ -14,8 +14,9 @@
 STEP, LOS, SUBS = 16, 4, 8
 STRETCH = STEP * LOS
 GROUPS, PER = 4, 4
-PIECES = 4
+PIECES = 2
 PIECE = ROWS // PIECES
+HOPS = ((0, 1), (0, 4), (1, 1), (2, 1), (4, 1), (4, 2), (4, 3))
 FIRST, CHUNK, WIDE, DEVICE, COLUMN, GAIN = range(6)
 
 
@@ -31,17 +32,21 @@
 
 
 def kernel(
-    q_ref,
-    k_ref,
-    v_ref,
-    g_ref,
-    w_ref,
+    q_hbm,
+    k_hbm,
+    v_hbm,
+    g_hbm,
+    w_hbm,
     par_ref,
     skip_ref,
     out_ref,
     gq_ref,
     gk_ref,
     gv_ref,
+    q_ref,
+    k_ref,
+    v_ref,
+    g_ref,
     mixed,
     grad_in,
     conv,
@@ -61,6 +66,7 @@
     weights,
     gated,
     total,
+    in_sem,
     w_send_z,
     w_send_x,
     w_recv,
@@ -71,12 +77,23 @@
     g_send,
     f_send,
     g_recv,
+    c_recv,
 ):
     ctx = lax.axis_index("ctx")
     tp = lax.axis_index("tp")
     zlo, x = lax.div(ctx, NX), lax.rem(ctx, NX)
     zhi, y, core = lax.div(tp, 2 * NY), lax.rem(lax.div(tp, 2), NY), lax.rem(tp, 2)
 
+    loads = [
+        pltpu.make_async_copy(src, dst, in_sem.at[n])
+        for n, (src, dst) in enumerate(
+            [(k_hbm, k_ref), (v_hbm, v_ref), (q_hbm, q_ref), (g_hbm, g_ref)]
+            + [(w_hbm, weights.at[ctx])]
+        )
+    ]
+    for load in loads:
+        load.start()
+
     def at_x(step):
         return (zlo * NX + lax.rem(x + step, NX), tp)
 
@@ -97,7 +114,6 @@
     partners += [at_y(i) for i in range(1, NY)] + [far, sibling]
     for partner in partners:
         pl.semaphore_signal(barrier, inc=1, device_id=partner, device_id_type=MESH)
-    pl.semaphore_wait(barrier, len(partners))
 
     def copy(src, dst, send, recv, device):
         return pltpu.make_async_remote_copy(
@@ -105,11 +121,12 @@
             device_id=device, device_id_type=MESH,
         )
 
-    def w_copy_z(step, right):
-        block = (zlo - step if right else zlo + step) * NX + x
+    def w_copy_z(n, right):
+        away, hop = HOPS[n]
+        block = (zlo - away if right else zlo + away) * NX + x
         slot = weights.at[block]
-        to = (ctx + NX, tp) if right else (ctx - NX, tp)
-        return copy(slot, slot, w_send_z.at[0 if right else 1, step], w_recv.at[block], to)
+        to = (ctx + hop * NX, tp) if right else (ctx - hop * NX, tp)
+        return copy(slot, slot, w_send_z.at[0 if right else 1, n], w_recv.at[block], to)
 
     def w_copy_x(z, step):
         block = z * NX + x
@@ -120,30 +137,34 @@
         slot = weights.at[block]
         copy(slot, slot, w_send_x.at[0, 0], w_recv.at[block], at_x(1)).wait_recv()
 
-    def w_right(step):
-        return jnp.logical_and(zlo - step >= 0, zlo < NZ - 1)
-
-    def w_left(step):
-        return jnp.logical_and(zlo + step < NZ, zlo > 0)
-
-    def w_step(step):
-        if step:
-            @pl.when(zlo - step >= 0)
+    def w_right(n):
+        away, hop = HOPS[n]
+        return jnp.logical_and(zlo - away >= 0, zlo + hop < NZ)
+
+    def w_left(n):
+        away, hop = HOPS[n]
+        return jnp.logical_and(zlo + away < NZ, zlo - hop >= 0)
+
+    def w_arrived(step):
+        @pl.when(zlo - step >= 0)
+        def _():
+            w_wait_recv((zlo - step) * NX + x)
+
+        @pl.when(zlo + step < NZ)
+        def _():
+            w_wait_recv((zlo + step) * NX + x)
+
+    def w_step(*which):
+        for n in which:
+            @pl.when(w_right(n))
             def _():
-                w_wait_recv((zlo - step) * NX + x)
-
-            @pl.when(zlo + step < NZ)
+                w_copy_z(n, True).start()
+
+            @pl.when(w_left(n))
             def _():
-                w_wait_recv((zlo + step) * NX + x)
-
-        @pl.when(w_right(step))
-        def _():
-            w_copy_z(step, True).start()
-
-        @pl.when(w_left(step))
-        def _():
-            w_copy_z(step, False).start()
-
+                w_copy_z(n, False).start()
+
+    def w_spread(step):
         @pl.when(zlo - step >= 0)
         def _():
             for i in range(1, NX):
@@ -154,9 +175,6 @@
             def _():
                 for i in range(1, NX):
                     w_copy_x(zlo + step, i).start()
-
-    weights[ctx] = w_ref[...]
-    w_step(0)
 
     def make_tables(h):
         def group(mg, acc):
@@ -306,7 +324,7 @@
         for r0 in range(0, ROWS, 128):
             rows = pl.ds(r0, 128)
             summed = conv[h, rows].astype(BF16).astype(F32) + skip * mixed[h, rows]
-            gated[tp, h, rows] = (q_ref[rows, lanes(h)].astype(F32) * summed).astype(BF16)
+            gated[zhi, core, y, h, rows] = (q_ref[rows, lanes(h)].astype(F32) * summed).astype(BF16)
             gq_ref[rows, lanes(h)] = (g_ref[rows, lanes(h)].astype(F32) * summed).astype(BF16)
 
     def gate_backward(h):
@@ -319,6 +337,9 @@
 
     for h in range(HALVES):
         make_tables(h)
+    for load in loads[:-1]:
+        load.wait()
+    for h in range(HALVES):
         prepare_rows(h)
 
     def forward_states(index, carry):
@@ -332,6 +353,11 @@
     lax.fori_loop(0, HALVES * GROUPS, forward_states, 0)
     lax.fori_loop(0, HALVES * GROUPS, backward_states, 0)
     lax.fori_loop(0, HALVES * GROUPS, make_wide, 0)
+    for h in range(HALVES):
+        inside(False, mixed, h)
+        inside(True, grad_in, h)
+    loads[-1].wait()
+    pl.semaphore_wait(barrier, len(partners))
 
     round_x = [
         copy(own_state.at[lax.rem(x + i, NX)], recv_x.at[x], s_send.at[0, i], x_recv.at[x], at_x(i))
@@ -340,8 +366,7 @@
     for c in round_x:
         c.start()
     recv_x[x] = own_state[x]
-    w_step(1)
-    inside(False, mixed, 0)
+    w_step(0, 1)
     for i in range(1, NX):
         src = lax.rem(x + NX - i, NX)
         copy(own_state.at[0], recv_x.at[src], s_send.at[0, i], x_recv.at[src], at_x(i)).wait_recv()
@@ -372,10 +397,9 @@
     for c in round_z:
         c.start()
     recv_z[zlo] = jnp.zeros_like(recv_z[zlo])
-    inside(False, mixed, 1)
+    w_spread(0)
+    w_arrived(1)
     w_step(2)
-    inside(True, grad_in, 0)
-    inside(True, grad_in, 1)
     for i in range(1, NZ):
         src = lax.rem(zlo + NZ - i, NZ)
         copy(column.at[0], recv_z.at[src], s_send.at[1, i], z_recv.at[src], at_z(i)).wait_recv()
@@ -403,16 +427,18 @@
     for c in round_p:
         c.start()
     entry_in[x] = prefix[x]
-    w_step(3)
+    w_arrived(2)
+    w_arrived(4)
+    w_step(3, 4, 5, 6)
     for i in range(1, NX):
         src = lax.rem(x + NX - i, NX)
         copy(prefix.at[0], entry_in.at[src], s_send.at[2, i], p_recv.at[src], at_x(i)).wait_recv()
 
-    def piece(block, h, n):
-        return gated.at[block, h, pl.ds(n * PIECE, PIECE)]
-
-    def half(block, h):
-        return gated.at[block, h]
+    def piece(side, yy, h, n):
+        return gated.at[side, core, yy, h, pl.ds(n * PIECE, PIECE)]
+
+    def half(side, yy, h):
+        return gated.at[side, core, yy, h]
 
     sends = []
 
@@ -421,80 +447,86 @@
         c.start()
         sends.append(c)
 
+    def send_far(h, n):
+        send(piece(zhi, y, h, n), g_send.at[h, n], g_recv.at[zhi, y, h, n], far)
+
     for h in range(HALVES):
         inject(False, h)
         gate_forward(h)
         for n in range(PIECES):
-            send(piece(tp, h, n), g_send.at[h, n], g_recv.at[tp, h, n], far)
+            send_far(h, n)
         for i in range(1, NY):
-            send(half(tp, h), g_send.at[h, PIECES + i - 1], g_recv.at[tp, h, 0], at_y(i))
-        send(half(tp, h), g_send.at[h, PIECES + 3], g_recv.at[tp, h, 0], sibling)
-        w_step(4 + h)
+            send(half(zhi, y, h), g_send.at[h, PIECES + i - 1], g_recv.at[zhi, y, h, 0], at_y(i))
+        w_spread(1 + h)
 
     for h in range(HALVES):
         inject(True, h)
         gate_backward(h)
+        w_spread(4 - h)
         if h == 0:
-            w_step(6)
-    w_step(7)
-
-    far_tp = far[1]
-
-    def wait_half(block, h):
-        copy(half(block, h), half(block, h), g_send.at[0, 0], g_recv.at[block, h, 0], far).wait_recv()
-
-    def wait_piece(block, h, n):
-        part = piece(block, h, n)
-        copy(part, part, g_send.at[0, 0], g_recv.at[block, h, n], far).wait_recv()
+            w_arrived(3)
+    for step in range(5, NZ):
+        w_arrived(step)
+        w_spread(step)
+
+    other = 1 - zhi
+
+    def arrived(part, recv):
+        copy(part, part, g_send.at[0, 0], recv, far).wait_recv()
 
     for h in range(HALVES):
         for i in range(1, NY):
-            block = tp_of(zhi, lax.rem(y + NY - i, NY), core)
-            wait_half(block, h)
-            send(half(block, h), f_send.at[0, h, i], g_recv.at[block, h, 0], sibling)
+            yy = lax.rem(y + i, NY)
+            arrived(half(zhi, yy, h), g_recv.at[zhi, yy, h, 0])
+        send(gated.at[zhi, core, :, h], f_send.at[0, h, 0], c_recv.at[0, h, 0], sibling)
 
     def pass_on(h, n):
-        wait_piece(far_tp, h, n)
+        part = piece(other, y, h, n)
+        arrived(part, g_recv.at[other, y, h, n])
         for i in range(1, NY):
-            to = at_y(i)
-            send(piece(far_tp, h, n), f_send.at[1 + n, h, i], g_recv.at[far_tp, h, n], to)
-        send(piece(far_tp, h, n), f_send.at[1 + n, h, 0], g_recv.at[far_tp, h, n], sibling)
+            send(part, f_send.at[1 + n, h, i], g_recv.at[other, y, h, n], at_y(i))
+
+    def along_y(h, n):
+        return gated.at[other, core, :, h, pl.ds(n * PIECE, PIECE)]
 
     def pass_core(h, n):
         for i in range(1, NY):
-            block = tp_of(1 - zhi, lax.rem(y + NY - i, NY), core)
-            wait_piece(block, h, n)
-            send(
-                piece(block, h, n), f_send.at[1 + PIECES + n, h, i], g_recv.at[block, h, n], sibling
-            )
+            yy = lax.rem(y + i, NY)
+            arrived(piece(other, yy, h, n), g_recv.at[other, yy, h, n])
+        send(along_y(h, n), f_send.at[1 + n, h, 0], c_recv.at[1, h, n], sibling)
 
     def near_product():
         for h in range(HALVES):
-            for i in range(NY):
-                wait_half(tp_of(zhi, i, 1 - core), h)
+            arrived(gated.at[zhi, 1 - core, :, h], c_recv.at[0, h, 0])
 
         for z in range(NZ):
             for i in range(1, NX):
                 w_wait_recv(z * NX + lax.rem(x + i, NX))
 
         def rows_of(n, carry):
-            rows = pl.ds(pl.multiple_of(n * PIECE, PIECE), PIECE)
+            rows = pl.ds(pl.multiple_of(n * 256, 256), 256)
             left = jnp.concatenate(
-                [gated[zhi * 8 + j, h, rows] for j in range(8) for h in range(HALVES)], axis=1
+                [
+                    gated[zhi, c, j, h, rows]
+                    for j in range(NY) for c in range(2) for h in range(HALVES)
+                ],
+                axis=1,
             )
             right = jnp.concatenate([weights[zhi * 16 + j] for j in range(16)], axis=0)
             total[rows] = jnp.dot(left, right, preferred_element_type=F32)
             return carry
 
-        lax.fori_loop(0, PIECES, rows_of, 0)
+        lax.fori_loop(0, ROWS // 256, rows_of, 0)
 
     def far_product(h, n):
-        for i in range(NY):
-            wait_piece(tp_of(1 - zhi, i, 1 - core), h, n)
-        first = (1 - zhi) * 8
+        part = gated.at[other, 1 - core, :, h, pl.ds(n * PIECE, PIECE)]
+        arrived(part, c_recv.at[1, h, n])
         rows = pl.ds(n * PIECE, PIECE)
-        left = jnp.concatenate([gated[first + j, h, rows] for j in range(8)], axis=1)
-        right = jnp.concatenate([weights[2 * (first + j) + h] for j in range(8)], axis=0)
+        pairs = [(j, c) for j in range(NY) for c in range(2)]
+        left = jnp.concatenate([gated[other, c, j, h, rows] for j, c in pairs], axis=1)
+        right = jnp.concatenate(
+            [weights[other * 16 + j * 4 + c * 2 + h] for j, c in pairs], axis=0
+        )
         summed = total[rows] + jnp.dot(left, right, preferred_element_type=F32)
         if h == HALVES - 1:
             out_ref[rows] = summed.astype(BF16)
@@ -502,7 +534,7 @@
             total[rows] = summed
 
     order = [(h, n) for h in range(HALVES) for n in range(PIECES)]
-    near_at = 5
+    near_at = 3
     for s in range(len(order) + 2):
         if s < len(order):
             pass_on(*order[s])
@@ -517,14 +549,14 @@
 
     for c in sends + round_x + round_z + round_p:
         c.wait_send()
-    for step in range(NZ):
-        @pl.when(w_right(step))
+    for n in range(len(HOPS)):
+        @pl.when(w_right(n))
         def _():
-            w_copy_z(step, True).wait_send()
-
-        @pl.when(w_left(step))
+            w_copy_z(n, True).wait_send()
+
+        @pl.when(w_left(n))
         def _():
-            w_copy_z(step, False).wait_send()
+            w_copy_z(n, False).wait_send()
 
     for z in range(NZ):
         for i in range(1, NX):
@@ -547,15 +579,16 @@
 
     vmem = pl.BlockSpec(memory_space=pltpu.VMEM)
     stream = jax.ShapeDtypeStruct((ROWS, HALVES * LANES), BF16)
-    blocks = lax.axis_size("tp")
+    hbm = pl.BlockSpec(memory_space=pl.ANY)
     sem = pltpu.SemaphoreType.DMA
     tile = (SUBS, LANES)
     return pl.pallas_call(
         kernel,
         out_shape=(stream,) * 4,
-        in_specs=[vmem] * 7,
+        in_specs=[hbm] * 5 + [vmem] * 2,
         out_specs=(vmem,) * 4,
         scratch_shapes=[
+            *[pltpu.VMEM((ROWS, HALVES * LANES), BF16)] * 4,
             pltpu.VMEM((HALVES, ROWS, LANES), F32),
             pltpu.VMEM((HALVES, ROWS, LANES), F32),
             pltpu.VMEM((HALVES, ROWS, LANES), F32),
@@ -573,9 +606,10 @@
             pltpu.VMEM((NX, HALVES, 4 * PER, LANES), F32),
             pltpu.VMEM((GROUPS, HALVES, 4 * PER, LANES), F32),
             pltpu.VMEM((NZ * NX, 128, HALVES * LANES), BF16),
-            pltpu.VMEM((blocks, HALVES, ROWS, LANES), BF16),
+            pltpu.VMEM((2, 2, NY, HALVES, ROWS, LANES), BF16),
             pltpu.VMEM((ROWS, HALVES * LANES), F32),
-            sem((2, NZ)),
+            sem((5,)),
+            sem((2, len(HOPS))),
             sem((NZ, NX)),
             sem((NZ * NX,)),
             sem((3, NZ)),
@@ -583,8 +617,9 @@
             sem((NZ,)),
             sem((NX,)),
             sem((HALVES, PIECES + 4)),
-            sem((1 + 2 * PIECES, HALVES, 4)),
-            sem((blocks, HALVES, PIECES)),
+            sem((1 + PIECES, HALVES, 4)),
+            sem((2, NY, HALVES, PIECES)),
+            sem((2, HALVES, PIECES)),
         ],
         compiler_params=pltpu.CompilerParams(
             collective_id=0, has_side_effects=True, vmem_limit_bytes=48 * 1024 * 1024

time: 100 us -> 82.5 us (0.82)
  Pallas kernels: 92.1 us -> 74.1 us
    pallas_call x1, Pallas kernels: 92.1 us -> 74.1 us  [body(): pl.pallas_call(kernel, out_shape=(stream,) * 4, in_specs=[hbm] * 5 + [vme...]
where the time goes in v2:
time: 82.5 us; the launch traced here: 81.7 us
  Pallas kernels  74.1 us (90%)
  local copies, waits for them, and re-layouts  6.1 us (7%)
    pallas_call x1, Pallas kernels, body(): pl.pallas_call(kernel, out_shape=(stream,) * 4, in_specs=[hbm] * 5 + [vme...  74.1 us
    unnamed x22, local copies, waits for them, and re-layouts  5.31 us

profile of v2, /device:TPU:1, one launch (start us, length us, event | category | flops | bytes accessed | tf_op | source)
XLA Modules:
  0.0 81.7 jit_solution(2210869571288755581)
XLA Ops:
  0.6 0.0 copy-start.6
  0.6 0.0 copy-start.7
  0.7 0.0 copy-start.8
  0.7 0.7 reshape.25
  1.4 0.0 copy-start.2
  1.5 0.0 copy-done.6
  1.5 0.0 copy-done.7
  1.5 0.0 copy-done.8
  1.5 0.0 copy-start
  1.6 0.0 copy-start.1
  1.6 0.7 fusion
  2.2 0.0 copy-start.5
  2.3 0.1 copy-done.2
  2.4 0.1 copy-done
  2.5 0.1 copy-done.1
  2.6 0.4 copy-done.5
  3.0 0.0 copy-start.3
  3.0 0.9 %copy-done.3 = bf16[512,256]{1,0:T(8,128)(2,1)S(1)} copy-done((bf16[512,256]{1,0:T(8,128)(2,1)S(1)}, bf16[512,256]{1,0:T(8,128)(2,1)}, u32[]{:S(2)}) %copy-start.3) | copy-done | bytes 262168
  3.9 0.0 copy-start.4
  3.9 0.8 %copy-done.4 = bf16[128,256]{1,0:T(8,128)(2,1)S(1)} copy-done((bf16[128,256]{1,0:T(8,128)(2,1)S(1)}, bf16[128,256]{1,0:T(8,128)(2,1)}, u32[]{:S(2)}) %copy-start.4) | copy-done | bytes 65560
  4.8 74.1 %shard_map.129 = (bf16[512,256]{1,0:T(8,128)(2,1)S(1)}, bf16[512,256]{1,0:T(8,128)(2,1)S(1)}, bf16[512,256]{1,0:T(8,128)(2,1)S(1)}, bf16[512,256]{1,0:T(8,128)(2,1)S(1)}) custom-call(bf16[512,256]{1,0:T(8,128)(2,1)S(1)} %copy-done, bf16[512,256]{1,0:T(8,128)(2,1)S(1)} %copy-done.1, bf16[512,256]{1,0:T(8,128)(2,1)S(1)} %copy-done.2, ...), custom_call_target="tpu_custom_call" | custom-call | tf_op jit(solution)/shard_map/pallas_call | solution.py:585
  78.9 0.7 copy.27
  79.6 0.7 copy.28
  80.3 0.7 copy.29
  81.0 0.7 copy.30
  (6 shorter events, 0.1 us)
Async XLA Ops:
  0.6 0.8 %copy-start.6 = (f32[256,16]{0,1:T(8,128)S(1)}, f32[256,16]{0,1:T(8,128)}, u32[]{:S(2)}) copy-start(f32[256,16]{0,1:T(8,128)} %param.14) | copy-start | bytes 49156
  0.6 0.8 %copy-start.7 = (f32[256,16]{0,1:T(8,128)S(1)}, f32[256,16]{0,1:T(8,128)}, u32[]{:S(2)}) copy-start(f32[256,16]{0,1:T(8,128)} %param.15) | copy-start | bytes 49156
  0.7 0.9 %copy-start.8 = (f32[5]{0:T(128)S(1)}, f32[5]{0:T(128)}, u32[]{:S(2)}) copy-start(f32[5]{0:T(128)} %constant.2.clone) | copy-start | bytes 64
  1.4 1.0 %copy-start.2 = (bf16[512,256]{1,0:T(8,128)(2,1)S(1)}, bf16[512,256]{1,0:T(8,128)(2,1)}, u32[]{:S(2)}) copy-start(bf16[512,256]{1,0:T(8,128)(2,1)} %v_hbm.1) | copy-start | bytes 786436
  1.5 1.0 %copy-start = (bf16[512,256]{1,0:T(8,128)(2,1)S(1)}, bf16[512,256]{1,0:T(8,128)(2,1)}, u32[]{:S(2)}) copy-start(bf16[512,256]{1,0:T(8,128)(2,1)} %q_hbm.1) | copy-start | bytes 786436
  1.6 1.0 %copy-start.1 = (bf16[512,256]{1,0:T(8,128)(2,1)S(1)}, bf16[512,256]{1,0:T(8,128)(2,1)}, u32[]{:S(2)}) copy-start(bf16[512,256]{1,0:T(8,128)(2,1)} %k_hbm.1) | copy-start | bytes 786436
  2.2 0.7 copy-start.5
  3.0 0.9 %copy-start.3 = (bf16[512,256]{1,0:T(8,128)(2,1)S(1)}, bf16[512,256]{1,0:T(8,128)(2,1)}, u32[]{:S(2)}) copy-start(bf16[512,256]{1,0:T(8,128)(2,1)} %g_hbm.1) | copy-start | bytes 786436
  3.9 0.8 %copy-start.4 = (bf16[128,256]{1,0:T(8,128)(2,1)S(1)}, bf16[128,256]{1,0:T(8,128)(2,1)}, u32[]{:S(2)}) copy-start(bf16[128,256]{1,0:T(8,128)(2,1)} %w_hbm.1) | copy-start | bytes 196612

commit v3 on v2

--- a/solution.py
+++ b/solution.py
@@ -352,10 +352,6 @@
 
     lax.fori_loop(0, HALVES * GROUPS, forward_states, 0)
     lax.fori_loop(0, HALVES * GROUPS, backward_states, 0)
-    lax.fori_loop(0, HALVES * GROUPS, make_wide, 0)
-    for h in range(HALVES):
-        inside(False, mixed, h)
-        inside(True, grad_in, h)
     loads[-1].wait()
     pl.semaphore_wait(barrier, len(partners))
 
@@ -367,6 +363,8 @@
         c.start()
     recv_x[x] = own_state[x]
     w_step(0, 1)
+    for h in range(HALVES):
+        inside(False, mixed, h)
     for i in range(1, NX):
         src = lax.rem(x + NX - i, NX)
         copy(own_state.at[0], recv_x.at[src], s_send.at[0, i], x_recv.at[src], at_x(i)).wait_recv()
@@ -400,6 +398,11 @@
     w_spread(0)
     w_arrived(1)
     w_step(2)
+    w_arrived(4)
+    w_step(4, 5, 6)
+    lax.fori_loop(0, HALVES * GROUPS, make_wide, 0)
+    for h in range(HALVES):
+        inside(True, grad_in, h)
     for i in range(1, NZ):
         src = lax.rem(zlo + NZ - i, NZ)
         copy(column.at[0], recv_z.at[src], s_send.at[1, i], z_recv.at[src], at_z(i)).wait_recv()
@@ -428,8 +431,7 @@
         c.start()
     entry_in[x] = prefix[x]
     w_arrived(2)
-    w_arrived(4)
-    w_step(3, 4, 5, 6)
+    w_step(3)
     for i in range(1, NX):
         src = lax.rem(x + NX - i, NX)
         copy(prefix.at[0], entry_in.at[src], s_send.at[2, i], p_recv.at[src], at_x(i)).wait_recv()
@@ -495,13 +497,16 @@
             arrived(piece(other, yy, h, n), g_recv.at[other, yy, h, n])
         send(along_y(h, n), f_send.at[1 + n, h, 0], c_recv.at[1, h, n], sibling)
 
+    def w_rows(side):
+        for z in range(NZ // 2):
+            for i in range(1, NX):
+                w_wait_recv((side * (NZ // 2) + z) * NX + lax.rem(x + i, NX))
+
     def near_product():
         for h in range(HALVES):
             arrived(gated.at[zhi, 1 - core, :, h], c_recv.at[0, h, 0])
 
-        for z in range(NZ):
-            for i in range(1, NX):
-                w_wait_recv(z * NX + lax.rem(x + i, NX))
+        w_rows(zhi)
 
         def rows_of(n, carry):
             rows = pl.ds(pl.multiple_of(n * 256, 256), 256)
@@ -534,17 +539,19 @@
             total[rows] = summed
 
     order = [(h, n) for h in range(HALVES) for n in range(PIECES)]
-    near_at = 3
+    near_at = 1
     for s in range(len(order) + 2):
         if s < len(order):
             pass_on(*order[s])
         if s == near_at:
             near_product()
-            for t in range(s - 1):
-                far_product(*order[t])
+            w_rows(other)
         if 1 <= s <= len(order):
             pass_core(*order[s - 1])
-        if s > near_at:
+        if s == near_at:
+            for t in range(max(s - 1, 0)):
+                far_product(*order[t])
+        elif s > near_at and s >= 2:
             far_product(*order[s - 2])
 
     for c in sends + round_x + round_z + round_p:

time: 82.5 us -> 80.8 us (0.979)
  the two profiles are of different devices: /device:TPU:1 before, /device:TPU:37 now
where the time goes in v3:
time: 80.8 us; the launch traced here: 80.5 us
  Pallas kernels  72.9 us (90%)
  local copies, waits for them, and re-layouts  6.1 us (8%)
    pallas_call x1, Pallas kernels, body(): pl.pallas_call(kernel, out_shape=(stream,) * 4, in_specs=[hbm] * 5 + [vme...  72.9 us
    unnamed x22, local copies, waits for them, and re-layouts  5.31 us

profile of v3, /device:TPU:37, one launch (start us, length us, event | category | flops | bytes accessed | tf_op | source)
XLA Modules:
  0.0 80.5 jit_solution(5264618477197433297)
XLA Ops:
  0.6 0.0 copy-start.6
  0.6 0.0 copy-start.7
  0.7 0.0 copy-start.8
  0.7 0.7 reshape.25
  1.4 0.0 copy-start.2
  1.5 0.0 copy-done.6
  1.5 0.0 copy-done.7
  1.5 0.0 copy-done.8
  1.5 0.0 copy-start
  1.6 0.0 copy-start.1
  1.6 0.7 fusion
  2.2 0.0 copy-start.5
  2.3 0.1 copy-done.2
  2.4 0.1 copy-done
  2.5 0.1 copy-done.1
  2.6 0.4 copy-done.5
  3.0 0.0 copy-start.3
  3.0 0.9 %copy-done.3 = bf16[512,256]{1,0:T(8,128)(2,1)S(1)} copy-done((bf16[512,256]{1,0:T(8,128)(2,1)S(1)}, bf16[512,256]{1,0:T(8,128)(2,1)}, u32[]{:S(2)}) %copy-start.3) | copy-done | bytes 262168
  3.9 0.0 copy-start.4
  3.9 0.8 %copy-done.4 = bf16[128,256]{1,0:T(8,128)(2,1)S(1)} copy-done((bf16[128,256]{1,0:T(8,128)(2,1)S(1)}, bf16[128,256]{1,0:T(8,128)(2,1)}, u32[]{:S(2)}) %copy-start.4) | copy-done | bytes 65560
  4.8 72.9 %shard_map.129 = (bf16[512,256]{1,0:T(8,128)(2,1)S(1)}, bf16[512,256]{1,0:T(8,128)(2,1)S(1)}, bf16[512,256]{1,0:T(8,128)(2,1)S(1)}, bf16[512,256]{1,0:T(8,128)(2,1)S(1)}) custom-call(bf16[512,256]{1,0:T(8,128)(2,1)S(1)} %copy-done, bf16[512,256]{1,0:T(8,128)(2,1)S(1)} %copy-done.1, bf16[512,256]{1,0:T(8,128)(2,1)S(1)} %copy-done.2, ...), custom_call_target="tpu_custom_call" | custom-call | tf_op jit(solution)/shard_map/pallas_call | solution.py:592
  77.7 0.7 copy.27
  78.4 0.7 copy.28
  79.1 0.7 copy.29
  79.8 0.7 copy.30
  (6 shorter events, 0.1 us)
Async XLA Ops:
  0.6 0.8 %copy-start.6 = (f32[256,16]{0,1:T(8,128)S(1)}, f32[256,16]{0,1:T(8,128)}, u32[]{:S(2)}) copy-start(f32[256,16]{0,1:T(8,128)} %param.14) | copy-start | bytes 49156
  0.6 0.8 %copy-start.7 = (f32[256,16]{0,1:T(8,128)S(1)}, f32[256,16]{0,1:T(8,128)}, u32[]{:S(2)}) copy-start(f32[256,16]{0,1:T(8,128)} %param.15) | copy-start | bytes 49156
  0.7 0.9 %copy-start.8 = (f32[5]{0:T(128)S(1)}, f32[5]{0:T(128)}, u32[]{:S(2)}) copy-start(f32[5]{0:T(128)} %constant.2.clone) | copy-start | bytes 64
  1.4 1.0 %copy-start.2 = (bf16[512,256]{1,0:T(8,128)(2,1)S(1)}, bf16[512,256]{1,0:T(8,128)(2,1)}, u32[]{:S(2)}) copy-start(bf16[512,256]{1,0:T(8,128)(2,1)} %v_hbm.1) | copy-start | bytes 786436
  1.5 1.0 %copy-start = (bf16[512,256]{1,0:T(8,128)(2,1)S(1)}, bf16[512,256]{1,0:T(8,128)(2,1)}, u32[]{:S(2)}) copy-start(bf16[512,256]{1,0:T(8,128)(2,1)} %q_hbm.1) | copy-start | bytes 786436
  1.6 1.0 %copy-start.1 = (bf16[512,256]{1,0:T(8,128)(2,1)S(1)}, bf16[512,256]{1,0:T(8,128)(2,1)}, u32[]{:S(2)}) copy-start(bf16[512,256]{1,0:T(8,128)(2,1)} %k_hbm.1) | copy-start | bytes 786436
  2.2 0.7 copy-start.5
  3.0 0.9 %copy-start.3 = (bf16[512,256]{1,0:T(8,128)(2,1)S(1)}, bf16[512,256]{1,0:T(8,128)(2,1)}, u32[]{:S(2)}) copy-start(bf16[512,256]{1,0:T(8,128)(2,1)} %g_hbm.1) | copy-start | bytes 786436
  3.9 0.8 %copy-start.4 = (bf16[128,256]{1,0:T(8,128)(2,1)S(1)}, bf16[128,256]{1,0:T(8,128)(2,1)}, u32[]{:S(2)}) copy-start(bf16[128,256]{1,0:T(8,128)(2,1)} %w_hbm.1) | copy-start | bytes 196612
